TPU v7x, 32 devices: a whole 2x2x4 slice. The times are simulated.
32 devices in a mesh: batch: 2 (over x), height: 4 (over y, core), width: 4 (over z).
Axes of the slice: x: 2, y: 2, z: 4, core: 2. Of those that a mesh axis runs over, the one named last changes fastest.
Arguments:
- image_query: bfloat16 [128, 32, 3072], P(('batch', 'height'), 'width'), parts along dimension 0, may hold values from -60 to 60
- image_key: bfloat16 [128, 32, 3072], P(('batch', 'height'), 'width'), parts along dimension 0, may hold values from -6 to 6
- image_value: bfloat16 [128, 32, 3072], P(('batch', 'height'), 'width'), parts along dimension 0, may hold values from -6 to 6
- text_query: bfloat16 [512, 3072], P(('batch', 'width')), parts along dimension 0, may hold values from -60 to 60
- text_key: bfloat16 [512, 3072], P(('batch', 'width')), parts along dimension 0, may hold values from -6 to 6
- text_value: bfloat16 [512, 3072], P(('batch', 'width')), parts along dimension 0, may hold values from -6 to 6
- text_length: int32 [2], P('batch'), parts along dimension 0, may hold values from 64 to 256
Outputs:
- image_out: bfloat16 [128, 32, 3072], P(('batch', 'height'), 'width'), parts along dimension 0
- text_out: bfloat16 [512, 3072], P(('batch', 'width')), parts along dimension 0
There are 2 independent parts, one for each index of `batch`. A program takes and returns all parts, laid end to end along the dimension named above; each array names one. Nothing has to cross between parts.
All inputs are finite; a program needn't handle non-finite values.
Results may differ from a plain program's by a relative error of at most 0.0034.
Values may be sent and summed in bfloat16 or wider, within the bound.
A program may use at most 128 MiB of HBM per device.

v0:
```python
import math

import jax
import jax.numpy as jnp
from jax import lax
from jax.sharding import PartitionSpec as P

HEAD_DIM = 128
RADIUS = 8


masked_score = -1e30


def padded(cells, sides, width):
    for axis, dim in sides:
        count = lax.axis_size(axis)
        ends = count - 1
        head = lax.slice_in_dim(cells, 0, width, axis=dim)
        tail = lax.slice_in_dim(cells, cells.shape[dim] - width, cells.shape[dim], axis=dim)
        cells = jnp.concatenate(
            [
                lax.ppermute(tail, axis, [(i, (i + 1) % count) for i in range(ends)]),
                cells,
                lax.ppermute(head, axis, [((i + 1) % count, i) for i in range(ends)]),
            ],
            axis=dim,
        )
    return cells


def group_attend(
    queries, win_keys, win_values, win_allowed, text_keys, text_values, text_allowed, score_scale
):
    score_win = (
        jnp.einsum("qhe,khe->hqk", queries, win_keys, preferred_element_type=jnp.float32)
        * score_scale
    )
    score_win = jnp.where(win_allowed[None], score_win, masked_score)
    score_text = (
        jnp.einsum("qhe,khe->hqk", queries, text_keys, preferred_element_type=jnp.float32)
        * score_scale
    )
    score_text = jnp.where(text_allowed[None, None], score_text, masked_score)
    row_peak = jnp.maximum(jnp.max(score_win, axis=-1), jnp.max(score_text, axis=-1))
    weight_win = jnp.exp(score_win - row_peak[..., None])
    weight_text = jnp.exp(score_text - row_peak[..., None])
    row_total = jnp.sum(weight_win, axis=-1) + jnp.sum(weight_text, axis=-1)
    numerator = jnp.einsum(
        "hqk,khe->qhe",
        weight_win.astype(jnp.bfloat16),
        win_values,
        preferred_element_type=jnp.float32,
    )
    numerator = numerator + jnp.einsum(
        "hqk,khe->qhe",
        weight_text.astype(jnp.bfloat16),
        text_values,
        preferred_element_type=jnp.float32,
    )
    return (numerator / jnp.transpose(row_total)[:, :, None]).astype(jnp.bfloat16)


def shards(image_query, image_key, image_value, text_query, text_key, text_value, text_length):
    tile_rows, tile_cols, width_all = image_query.shape
    head_count = width_all // HEAD_DIM
    query_count = tile_rows * tile_cols
    score_scale = 1.0 / math.sqrt(HEAD_DIM)
    stacked = jnp.stack((image_key, image_value))
    extended = padded(stacked, (("height", 1), ("width", 2)), RADIUS)
    all_query, all_key, all_value = (
        lax.all_gather(text_query, "width", axis=0, tiled=True),
        lax.all_gather(text_key, "width", axis=0, tiled=True),
        lax.all_gather(text_value, "width", axis=0, tiled=True),
    )
    text_count = all_query.shape[0]
    text_allowed = jnp.arange(text_count, dtype=jnp.int32) < text_length[0]
    ext_rows = tile_rows + 2 * RADIUS
    ext_cols = tile_cols + 2 * RADIUS
    window_keys = extended[0].reshape(ext_rows * ext_cols, head_count, HEAD_DIM)
    window_values = extended[1].reshape(ext_rows * ext_cols, head_count, HEAD_DIM)
    row_base = lax.axis_index("height") * tile_rows
    col_base = lax.axis_index("width") * tile_cols
    grid_rows = tile_rows * lax.axis_size("height")
    grid_cols = tile_cols * lax.axis_size("width")
    query_row = jnp.arange(tile_rows, dtype=jnp.int32)[:, None, None, None]
    query_col = jnp.arange(tile_cols, dtype=jnp.int32)[None, :, None, None]
    key_row = jnp.arange(ext_rows, dtype=jnp.int32)[None, None, :, None]
    key_col = jnp.arange(ext_cols, dtype=jnp.int32)[None, None, None, :]
    delta_row = key_row - RADIUS - query_row
    delta_col = key_col - RADIUS - query_col
    global_row = row_base + key_row - RADIUS
    global_col = col_base + key_col - RADIUS
    inside = (
        (global_row >= 0) & (global_row < grid_rows) & (global_col >= 0) & (global_col < grid_cols)
    )
    near = delta_row * delta_row + delta_col * delta_col <= RADIUS * RADIUS
    win_allowed = (near & inside).reshape(query_count, ext_rows * ext_cols)
    query_heads = image_query.reshape(query_count, head_count, HEAD_DIM)
    text_key_heads = all_key.reshape(text_count, head_count, HEAD_DIM)
    text_value_heads = all_value.reshape(text_count, head_count, HEAD_DIM)
    group_heads = math.gcd(head_count, 6)
    group_count = head_count // group_heads

    def latent_group(group_index):
        head_start = group_index * group_heads

        def select_heads(source):
            return lax.dynamic_slice_in_dim(source, head_start, group_heads, 1)

        return group_attend(
            select_heads(query_heads),
            select_heads(window_keys),
            select_heads(window_values),
            win_allowed,
            select_heads(text_key_heads),
            select_heads(text_value_heads),
            text_allowed,
            score_scale,
        )

    groups = lax.map(latent_group, jnp.arange(group_count, dtype=jnp.int32))
    image_out = jnp.transpose(groups, (1, 0, 2, 3)).reshape(tile_rows, tile_cols, width_all)
    text_query_heads = all_query.reshape(text_count, head_count, HEAD_DIM)
    own_key_heads = image_key.reshape(query_count, head_count, HEAD_DIM)
    own_value_heads = image_value.reshape(query_count, head_count, HEAD_DIM)
    image_scores = (
        jnp.einsum(
            "the,khe->htk", text_query_heads, own_key_heads, preferred_element_type=jnp.float32
        )
        * score_scale
    )
    local_peak = jnp.max(image_scores, axis=-1)
    owner_rows = text_query.shape[0]
    owner_start = lax.axis_index("width") * owner_rows
    owner_heads = text_query.reshape(owner_rows, head_count, HEAD_DIM)
    text_scores = (
        jnp.einsum("the,khe->htk", owner_heads, text_key_heads, preferred_element_type=jnp.float32)
        * score_scale
    )
    text_scores = jnp.where(text_allowed[None, None], text_scores, masked_score)
    owner_peak = jnp.max(text_scores, axis=-1)
    present = lax.dynamic_slice_in_dim(local_peak, owner_start, owner_rows, 1)
    local_peak = lax.dynamic_update_slice_in_dim(
        local_peak, jnp.maximum(present, owner_peak), owner_start, 1
    )
    global_peak = lax.pmax(local_peak, ("height", "width"))
    image_weight = jnp.exp(image_scores - global_peak[..., None])
    image_total = jnp.sum(image_weight, axis=-1)
    image_rounded = image_weight.astype(jnp.bfloat16)
    partial_numer = jnp.einsum(
        "htk,khe->the", image_rounded, own_value_heads, preferred_element_type=jnp.float32
    ).reshape(text_count, width_all)
    partial_total = jnp.transpose(image_total)
    piece_numer, piece_total = (
        lax.psum_scatter(partial_numer, "width", scatter_dimension=0, tiled=True),
        lax.psum_scatter(partial_total, "width", scatter_dimension=0, tiled=True),
    )
    summed_numer, summed_total = lax.psum((piece_numer, piece_total), "height")
    owner_global = lax.dynamic_slice_in_dim(global_peak, owner_start, owner_rows, 1)
    text_weight = jnp.exp(text_scores - owner_global[..., None])
    text_total = jnp.sum(text_weight, axis=-1)
    text_numer = jnp.einsum(
        "htk,khe->the",
        text_weight.astype(jnp.bfloat16),
        text_value_heads,
        preferred_element_type=jnp.float32,
    )
    numerator = summed_numer.reshape(owner_rows, head_count, HEAD_DIM) + text_numer
    denominator = summed_total + jnp.transpose(text_total)
    text_out = (
        (numerator / denominator[:, :, None]).astype(jnp.bfloat16).reshape(owner_rows, width_all)
    )
    return (image_out, text_out)


def solution(mesh):
    in_specs = (
        P(("batch", "height"), "width", None),
        P(("batch", "height"), "width", None),
        P(("batch", "height"), "width", None),
        P(("batch", "width"), None),
        P(("batch", "width"), None),
        P(("batch", "width"), None),
        P("batch"),
    )
    out_specs = (P(("batch", "height"), "width", None), P(("batch", "width"), None))
    return jax.shard_map(shards, mesh=mesh, in_specs=in_specs, out_specs=out_specs, check_vma=False)
```

profile of v0, /device:TPU:0, one launch (start us, length us, event | category | flops | bytes accessed | tf_op | source)
XLA Modules:
  0.0 384.2 jit_solution(9155463635395113892)
XLA Ops:
  9.5 2.7 fusion.62
  13.4 4.0 %collective-permute-start = (bf16[2,8,8,3072]{3,2,1,0:T(8,128)(2,1)}, bf16[2,8,8,3072]{3,2,1,0:T(8,128)(2,1)}, u32[]{:S(2)}, u32[]{:S(2)}) collective-permute-start(bf16[2,8,8,3072]{3,2,1,0:T(8,128)(2,1)} %get-tuple-element.152), channel_id=1, source_target_pairs={{0,4},{4,8},{8,12},{1,5},{5,9},{9,13},{2,6},{6,10},{10,14},{3,7},{... | collective-permute-start | bytes 2359304 | tf_op jit(solution)/shard_map/ppermute | solution.py:23
  20.2 29.2 %all-gather.4.cloned.1.call-done = bf16[256,3072]{1,0:T(8,128)(2,1)} async-done(((bf16[64,3072]{1,0:T(8,128)(2,1)}), bf16[256,3072]{1,0:T(8,128)(2,1)}) %all-gather.4.cloned.1.call-update) | async-done | bytes 1572880 | tf_op jit(solution)/shard_map/all_gather | solution.py:73
  51.1 35.8 %all-gather.8.cloned.1.call-done = bf16[256,3072]{1,0:T(8,128)(2,1)} async-done(((bf16[64,3072]{1,0:T(8,128)(2,1)}), bf16[256,3072]{1,0:T(8,128)(2,1)}) %all-gather.8.cloned.1.call-update) | async-done | bytes 1572880 | tf_op jit(solution)/shard_map/all_gather | solution.py:72
  92.7 60.8 %pmax.7 = f32[24,256]{1,0:T(8,128)S(1)} all-reduce(f32[24,256]{1,0:T(8,128)S(1)} %dynamic_update_slice.7), channel_id=1, replica_groups=mesh['batch'=2,'height'=4,'width'=4] {'height','width'}, use_global_device_ids=true, to_apply=%region_8.9 | all-reduce | flops 6144 | bytes 49152 | tf_op jit(solution)/shard_map/pmax | solution.py:147
  154.9 3.6 fusion.51
  158.5 3.5 copy.48
  163.4 3.1 pad_maximum_fusion.1
  167.8 6.2 %collective-permute-start.2 = (bf16[2,32,8,3072]{3,2,1,0:T(8,128)(2,1)}, bf16[2,32,8,3072]{3,2,1,0:T(8,128)(2,1)}, u32[]{:S(2)}, u32[]{:S(2)}) collective-permute-start(bf16[2,32,8,3072]{3,2,1,0:T(8,128)(2,1)} %pad_maximum_fusion.1), channel_id=1, source_target_pairs={{0,1},{1,2},{2,3},{4,5},{5,6},{6,7},{8,9},{9,10},{10,11},{12,13},{... | collective-permute-start | bytes 9437192 | tf_op jit(solution)/shard_map/ppermute | solution.py:23
  179.5 11.1 %psum.15 = f32[64,24]{0,1:T(8,128)S(1)} all-reduce(f32[64,24]{0,1:T(8,128)S(1)} %copy.57), channel_id=1, replica_groups=mesh['batch'=2,'height'=4,'width'=4] {'height'}, use_global_device_ids=true, to_apply=%region_13.14 | all-reduce | flops 1536 | bytes 12288 | tf_op jit(solution)/shard_map/psum | solution.py:159
  190.6 96.0 %collective-permute-done.3 = bf16[2,32,8,3072]{3,2,1,0:T(8,128)(2,1)} collective-permute-done((bf16[2,32,8,3072]{3,2,1,0:T(8,128)(2,1)}, bf16[2,32,8,3072]{3,2,1,0:T(8,128)(2,1)}, u32[]{:S(2)}, u32[]{:S(2)}) %collective-permute-start.3) | collective-permute-done | bytes 3145760 | tf_op jit(solution)/shard_map/ppermute | solution.py:25
  287.4 5.6 %pad_maximum_fusion = bf16[2,32,24,3072]{3,2,1,0:T(8,128)(2,1)S(1)} fusion(bf16[2,32,8,3072]{3,2,1,0:T(8,128)(2,1)} %collective-permute-done.3, bf16[2,8,8,3072]{3,2,1,0:T(8,128)(2,1)} %collective-permute-done.1, bf16[1,16,8,3072]{3,2,1,0:T(8,128)(2,1)} %bitcast.102, bf16[1,16,8,3072]{3,2,1,0:T(8,128)(2,1)} %bitcast.98, ...), kind=kLoop, calls=%fused_computation.41 | loop fusion | flops 56623104 | bytes 18874368 | tf_op jit(solution)/shard_map/concatenate | solution.py:21
  293.0 4.4 %fusion.73 = (bf16[1,32,24,3072]{3,2,1,0:T(8,128)(2,1)}, bf16[1,32,24,3072]{3,2,1,0:T(8,128)(2,1)}) fusion(bf16[2,32,24,3072]{3,2,1,0:T(8,128)(2,1)S(1)} %pad_maximum_fusion), kind=kLoop, calls=%fused_computation.86 | loop fusion | bytes 18874368 | tf_op jit(solution)/shard_map/slice | solution.py:80
  297.4 6.0 %copy.62 = bf16[96,8,24,128]{3,2,1,0:T(8,128)(2,1)} copy(bf16[96,8,24,128]{3,1,2,0:T(8,128)(2,1)} %bitcast.94) | data formatting | bytes 9437184
  303.4 7.0 %copy.36 = bf16[768,24,128]{0,2,1:T(8,128)(2,1)} copy(bf16[768,24,128]{2,1,0:T(8,128)(2,1)} %bitcast.91) | data formatting | bytes 9437184
  310.5 3.7 copy.64
  314.2 3.2 copy.38
  319.7 49.5 %while.11 = (s32[]{:T(128)}, bf16[4,128,6,128]{1,3,2,0:T(8,128)(2,1)}, s32[4]{0:T(128)S(1)}, bf16[768,24,128]{0,2,1:T(8,128)(2,1)}, bf16[128,24,128]{2,0,1:T(8,1...) while((s32[]{:T(128)}, ...), condition=%wide.region_5.6_spmd.clone, body=%wide.region_0.5_spmd.clone.sunk | while | flops 411106048 | bytes 14601703 | solution.py:122
  329.2 2.8 fusion.101
  341.6 2.8 fusion.101
  354.0 2.8 fusion.101
  366.3 2.8 fusion.101
  369.2 2.8 copy.40
  371.9 2.7 reshape.194
  (121 shorter events, 63.5 us)
Async XLA Ops:
  7.2 10.2 %copy-start.1 = (bf16[16,8,3072]{2,1,0:T(8,128)(2,1)S(1)}, bf16[16,8,3072]{2,1,0:T(8,128)(2,1)}, u32[]{:S(2)}) copy-start(bf16[16,8,3072]{2,1,0:T(8,128)(2,1)} %param.10) | copy-start | bytes 2359300
  7.2 42.2 %all-gather.4.cloned.1.call-start = ((), (), s32[]{:S(2)}) async-start(), calls=%async_computation.2 | async-start | bytes 1966080 | tf_op jit(solution)/shard_map/all_gather | solution.py:73
  7.9 79.1 %all-gather.8.cloned.1.call-start = ((), (), s32[]{:S(2)}) async-start(), calls=%async_computation.4 | async-start | bytes 1966080 | tf_op jit(solution)/shard_map/all_gather | solution.py:72
  8.7 166.7 %all-gather.6.cloned.1.call-start = ((), (), s32[]{:S(2)}) async-start(), calls=%async_computation.3 | async-start | bytes 1966080 | tf_op jit(solution)/shard_map/all_gather | solution.py:74
  9.4 169.2 %reduce-scatter.7.cloned.1.call-start = ((), (), s32[]{:S(2)}) async-start(), calls=%async_computation.7 | async-start | bytes 163840
  9.4 9.7 %copy-start.3 = (bf16[16,8,3072]{2,1,0:T(8,128)(2,1)S(1)}, bf16[16,8,3072]{2,1,0:T(8,128)(2,1)}, u32[]{:S(2)}) copy-start(bf16[16,8,3072]{2,1,0:T(8,128)(2,1)} %param.11) | copy-start | bytes 2359300
  12.2 150.0 %collective-permute-start.1 = (bf16[2,8,8,3072]{3,2,1,0:T(8,128)(2,1)}, bf16[2,8,8,3072]{3,2,1,0:T(8,128)(2,1)}, u32[]{:S(2)}, u32[]{:S(2)}) collective-permute-start(bf16[2,8,8,3072]{3,2,1,0:T(8,128)(2,1)} %get-tuple-element.153), channel_id=1, source_target_pairs={{4,0},{8,4},{12,8},{5,1},{9,5},{13,9},{6,2},{10,6},{14,10},{7,3},{... | collective-permute-start | bytes 2359304 | tf_op jit(solution)/shard_map/ppermute | solution.py:25
  13.4 148.7 %collective-permute-start = (bf16[2,8,8,3072]{3,2,1,0:T(8,128)(2,1)}, bf16[2,8,8,3072]{3,2,1,0:T(8,128)(2,1)}, u32[]{:S(2)}, u32[]{:S(2)}) collective-permute-start(bf16[2,8,8,3072]{3,2,1,0:T(8,128)(2,1)} %get-tuple-element.152), channel_id=1, source_target_pairs={{0,4},{4,8},{8,12},{1,5},{5,9},{9,13},{2,6},{6,10},{10,14},{3,7},{... | collective-permute-start | bytes 2359304 | tf_op jit(solution)/shard_map/ppermute | solution.py:23
  51.1 40.0 %copy-start = (bf16[256,3072]{0,1:T(8,128)(2,1)}, bf16[256,3072]{0,1:T(8,128)(2,1)S(1)}, u32[]{:S(2)}) copy-start(bf16[256,3072]{0,1:T(8,128)(2,1)S(1)} %copy.34) | copy-start | bytes 4718596
  51.1 38.4 %copy-start.11 = (bf16[64,3072]{1,0:T(8,128)(2,1)S(1)}, bf16[64,3072]{1,0:T(8,128)(2,1)}, u32[]{:S(2)}) copy-start(bf16[64,3072]{1,0:T(8,128)(2,1)} %param.12) | copy-start | bytes 1179652
  89.6 1.6 copy-start.9
  89.6 2.2 copy-start.10
  154.9 162.5 %reduce-scatter.5.cloned.1.call-start = ((), (), s32[]{:S(2)}) async-start(), calls=%async_computation.5 | async-start | bytes 3932160 | tf_op jit(solution)/shard_map/reduce_scatter | solution.py:156
  162.0 1.1 copy-start.2
  162.0 1.4 copy-start.4
  162.1 11.9 %copy-start.12 = (bf16[16,8,3072]{2,1,0:T(8,128)(2,1)S(1)}, bf16[16,8,3072]{2,1,0:T(8,128)(2,1)}, u32[]{:S(2)}) copy-start(bf16[16,8,3072]{2,1,0:T(8,128)(2,1)} %param.9) | copy-start | bytes 2359300
  162.1 212.6 %all-reduce.2.cloned.1.call-start = ((), (), s32[]{:S(2)}) async-start(), calls=%async_computation.6 | async-start | bytes 1572864 | tf_op jit(solution)/shard_map/psum | solution.py:159
  166.5 120.1 %collective-permute-start.3 = (bf16[2,32,8,3072]{3,2,1,0:T(8,128)(2,1)}, bf16[2,32,8,3072]{3,2,1,0:T(8,128)(2,1)}, u32[]{:S(2)}, u32[]{:S(2)}) collective-permute-start(bf16[2,32,8,3072]{3,2,1,0:T(8,128)(2,1)} %pad_maximum_fusion.1), channel_id=1, source_target_pairs={{1,0},{2,1},{3,2},{5,4},{6,5},{7,6},{9,8},{10,9},{11,10},{13,12},{... | collective-permute-start | bytes 9437192 | tf_op jit(solution)/shard_map/ppermute | solution.py:25
  167.8 119.6 %collective-permute-start.2 = (bf16[2,32,8,3072]{3,2,1,0:T(8,128)(2,1)}, bf16[2,32,8,3072]{3,2,1,0:T(8,128)(2,1)}, u32[]{:S(2)}, u32[]{:S(2)}) collective-permute-start(bf16[2,32,8,3072]{3,2,1,0:T(8,128)(2,1)} %pad_maximum_fusion.1), channel_id=1, source_target_pairs={{0,1},{1,2},{2,3},{4,5},{5,6},{6,7},{8,9},{9,10},{10,11},{12,13},{... | collective-permute-start | bytes 9437192 | tf_op jit(solution)/shard_map/ppermute | solution.py:23
  174.2 3.9 %copy-start.7 = (f32[24,64,256]{2,1,0:T(8,128)S(1)}, f32[24,64,256]{2,1,0:T(8,128)}, u32[]{:S(2)}) copy-start(f32[24,64,256]{2,1,0:T(8,128)} %get-tuple-element.157) | copy-start | bytes 4718596
  317.4 2.3 copy-start.5
  369.2 5.5 %copy-start.6 = (bf16[256,24,128]{0,2,1:T(8,128)(2,1)S(1)}, bf16[256,24,128]{0,2,1:T(8,128)(2,1)}, u32[]{:S(2)}) copy-start(bf16[256,24,128]{0,2,1:T(8,128)(2,1)} %get-tuple-element.297) | copy-start | bytes 4718596
  369.2 5.5 %copy-start.8 = (f32[24,64,256]{2,1,0:T(8,128)S(1)}, f32[24,64,256]{2,1,0:T(8,128)}, u32[]{:S(2)}) copy-start(f32[24,64,256]{2,1,0:T(8,128)} %get-tuple-element.157) | copy-start | bytes 4718596
Sparse Core Ops, SparseCore 0:
  9.6 39.7 all-gather.3
  51.0 35.9 all-gather.7
  88.5 37.1 all-gather.5
  155.0 16.5 reduce-scatter.6
  173.9 106.6 reduce-scatter.4
  319.8 35.9 all-reduce.1
where the time goes:
time: 386 us; the launch traced here: 384 us
  waiting for transfers between devices  164 us (42%)
  blocking collectives  71.9 us (19%)
  local copies, waits for them, and re-layouts  59 us (15%)
  matrix products  37.3 us (10%)
  other arithmetic  21.1 us (5%)
  between operations  15 us (4%)
  starting transfers between devices  13 us (3%)
    ppermute x2, waiting for transfers between devices, padded(): lax.ppermute(head, axis, [((i + 1) % count, i) for i in range(ends)])  96 us
    pmax x1, blocking collectives, shards(): global_peak = lax.pmax(local_peak, ('height', 'width'))  60.8 us
    all_gather x1, waiting for transfers between devices, shards(): lax.all_gather(text_query, 'width', axis=0, tiled=True)  35.8 us
    all_gather x1, waiting for transfers between devices, shards(): lax.all_gather(text_key, 'width', axis=0, tiled=True)  29.2 us
    unnamed x36, local copies, waits for them, and re-layouts  26.8 us
    dot_general x4, matrix products, group_attend(): jnp.einsum('hqk,khe->qhe', weight_win.astype(jnp.bfloat16), win_values, p...  11.4 us
    psum x1, blocking collectives, shards(): summed_numer, summed_total = lax.psum((piece_numer, piece_total), 'height')  11.1 us
    ppermute x2, starting transfers between devices, padded(): lax.ppermute(tail, axis, [(i, (i + 1) % count) for i in range(ends)])  10.2 us
  transfers between devices with their start and end apart: 10, of which 4 were waited for; matrix products, arithmetic and copies ran while one was open for 29% of the time, Pallas kernels for 0%

commit v1 on v0

v1 whole, which is shorter than its diff:
```python
import functools
import math

import jax
import jax.numpy as jnp
from jax import lax
from jax.experimental import pallas as pl
from jax.experimental.pallas import tpu as pltpu
from jax.sharding import PartitionSpec as P

HEAD_DIM = 128
RADIUS = 8
CHUNKS = 4
MASKED = -1e30
SCALE = math.log2(math.e) / math.sqrt(HEAD_DIM)
NT = (((1,), (1,)), ((), ()))


def dot_nt(a, b):
    return lax.dot_general(a, b, NT, preferred_element_type=jnp.float32)


def dot_nn(a, b):
    return jnp.dot(a, b, preferred_element_type=jnp.float32)


def joint(
    dims,
    length_ref,
    q_ref,
    k_hbm,
    v_hbm,
    tq_hbm,
    tk_hbm,
    tv_hbm,
    image_out,
    text_out,
    kbuf,
    vbuf,
    tk,
    tv,
    tq,
    xk,
    xv,
    obuf,
    rbuf,
    tout,
    bias,
    local_sem,
    zs,
    zr,
    vs,
    vr,
    ts,
    tr,
    ps,
    pr,
    qs,
    qr,
    xs,
    xr,
    os_,
    or_,
    fs,
    fr,
):
    n_h, n_w, rows, cols, heads, own_text, parts = dims
    tile = rows * cols
    strip = RADIUS * cols
    text = own_text * n_w
    groups = n_h // parts
    part_heads = heads // parts
    pc = part_heads * HEAD_DIM
    chunk_heads = heads // CHUNKS
    cc = chunk_heads * HEAD_DIM
    hc = cc // 2
    h = lax.axis_index("height")
    w = lax.axis_index("width")
    group = lax.div(h, parts)
    part = lax.rem(h, parts)
    par = lax.rem(h, 2)
    has_left, has_right = w > 0, w < n_w - 1
    has_up, has_down = h > 0, h < n_h - 1

    def at(hh, ww):
        return {"height": hh, "width": ww}

    def send(src, dst, s, r, device):
        return pltpu.make_async_remote_copy(
            src_ref=src,
            dst_ref=dst,
            send_sem=s,
            recv_sem=r,
            device_id=device,
            device_id_type=pl.DeviceIdType.MESH,
        )

    images = ((k_hbm, kbuf), (v_hbm, vbuf))
    texts = ((tk_hbm, tk), (tv_hbm, tv))
    part_cols = pl.ds(pl.multiple_of(part * pc, 128), pc)
    my_rows = pl.ds(pl.multiple_of(w * own_text, 16), own_text)

    barrier = pltpu.get_barrier_semaphore()
    greeted = 0
    for d in range(1, n_w):
        pl.semaphore_signal(barrier, inc=1, device_id=at(h, lax.rem(w + d, n_w)), device_id_type=pl.DeviceIdType.MESH)
        greeted += 1
    for d in range(1, n_h):
        pl.semaphore_signal(barrier, inc=1, device_id=at(lax.rem(h + d, n_h), w), device_id_type=pl.DeviceIdType.MESH)
        greeted += 1
    for g in range(1, groups):
        for d in range(1, n_w):
            pl.semaphore_signal(
                barrier,
                inc=1,
                device_id=at(lax.rem(h + g * parts, n_h), lax.rem(w + d, n_w)),
                device_id_type=pl.DeviceIdType.MESH,
            )
            greeted += 1
    pl.semaphore_wait(barrier, greeted)

    locals_ = []
    for i, (src, dst) in enumerate(images):
        locals_.append(pltpu.make_async_copy(src, dst.at[pl.ds(0, tile), :], local_sem.at[i]))
    locals_.append(pltpu.make_async_copy(tq_hbm.at[:, part_cols], tq.at[my_rows, :], local_sem.at[2]))
    my_slot = pl.ds(pl.multiple_of(part * tile, 16), tile)
    for i, (src, dst) in enumerate(((k_hbm, xk), (v_hbm, xv))):
        locals_.append(pltpu.make_async_copy(src.at[:, part_cols], dst.at[my_slot, :], local_sem.at[3 + i]))

    def half_cols(c):
        return pl.ds(pl.multiple_of(c * cc + par * hc, 128), hc)

    for c in range(CHUNKS):
        for i, (src, dst) in enumerate(texts):
            locals_.append(
                pltpu.make_async_copy(
                    src.at[:, half_cols(c)], dst.at[my_rows, half_cols(c)], local_sem.at[5 + 2 * c + i]
                )
            )
    for copy in locals_:
        copy.start()

    q_sends = [
        send(tq_hbm.at[:, part_cols], tq.at[my_rows, :], qs.at[d], qr.at[d], at(h, lax.rem(w + d, n_w)))
        for d in range(1, n_w)
    ]
    x_sends = []
    for d in range(1, parts):
        other = lax.rem(part + d, parts)
        other_cols = pl.ds(pl.multiple_of(other * pc, 128), pc)
        for i, (src, dst) in enumerate(((k_hbm, xk), (v_hbm, xv))):
            x_sends.append(
                send(src.at[:, other_cols], dst.at[my_slot, :], xs.at[d, i], xr.at[d, i], at(group * parts + other, w))
            )

    def text_sends(c):
        return [
            send(
                src.at[:, half_cols(c)],
                dst.at[my_rows, half_cols(c)],
                ts.at[c, d, i],
                tr.at[c, d, i],
                at(h, lax.rem(w + d, n_w)),
            )
            for d in range(1, n_w)
            for i, (src, dst) in enumerate(texts)
        ]

    def pair_sends(c):
        partner = h + 1 - 2 * par
        return [
            send(dst.at[:, half_cols(c)], dst.at[:, half_cols(c)], ps.at[c, i], pr.at[c, i], at(partner, w))
            for i, (_, dst) in enumerate(texts)
        ]

    def side_sends(c, way):
        to = w + 1 if way == 0 else w - 1
        columns = pl.ds(c * cc, cc)
        return [
            send(
                src.at[:, columns],
                dst.at[pl.ds(tile * (1 + way), tile), columns],
                zs.at[c, way, i],
                zr.at[c, way, i],
                at(h, to),
            )
            for i, (src, dst) in enumerate(images)
        ]

    def strip_sends(c, way, piece):
        to = h + 1 if way == 0 else h - 1
        columns = pl.ds(c * cc, cc)
        start = tile - strip if way == 0 else 0
        slot = 3 * tile + (3 * way + piece) * strip
        return [
            send(
                (src if piece == 0 else dst).at[pl.ds(piece * tile + start, strip), columns],
                dst.at[pl.ds(slot, strip), columns],
                vs.at[c, way, piece, i],
                vr.at[c, way, piece, i],
                at(to, w),
            )
            for i, (src, dst) in enumerate(images)
        ]

    side_out = (has_right, has_left)
    side_in = (has_left, has_right)
    strip_out = (has_down, has_up)
    strip_in = (has_up, has_down)
    piece_there = (True, has_left, has_right)

    def start_chunk(c):
        for copy in text_sends(c):
            copy.start()
        for way in range(2):

            @pl.when(side_out[way])
            def _(way=way):
                for copy in side_sends(c, way):
                    copy.start()

            @pl.when(strip_out[way])
            def _(way=way):
                for copy in strip_sends(c, way, 0):
                    copy.start()

    def relay_chunk(c):
        for copy in text_sends(c):
            copy.wait_recv()
        for i in range(2):
            locals_[5 + 2 * c + i].wait()
        for copy in pair_sends(c):
            copy.start()
        for way in range(2):

            @pl.when(side_in[way])
            def _(way=way):
                for copy in side_sends(c, way):
                    copy.wait_recv()
                for up in range(2):

                    @pl.when(strip_out[up])
                    def _():
                        for copy in strip_sends(c, up, 1 + way):
                            copy.start()

    def wait_chunk(c):
        for copy in pair_sends(c):
            copy.wait_recv()
        for way in range(2):
            for piece in range(3):

                @pl.when(strip_in[way] & piece_there[piece])
                def _(way=way, piece=piece):
                    for copy in strip_sends(c, way, piece):
                        copy.wait_recv()

    def finish_chunk(c):
        for copy in text_sends(c) + pair_sends(c):
            copy.wait_send()
        for way in range(2):

            @pl.when(side_out[way])
            def _(way=way):
                for copy in side_sends(c, way):
                    copy.wait_send()

            for piece in range(3):

                @pl.when(strip_out[way] & piece_there[piece])
                def _(way=way, piece=piece):
                    for copy in strip_sends(c, way, piece):
                        copy.wait_send()

    for copy in q_sends + x_sends:
        copy.start()
    start_chunk(0)
    start_chunk(1)

    def region(first, count, row_off, col_off, valid):
        key = lax.broadcasted_iota(jnp.int32, (tile, count), 1)
        query = lax.broadcasted_iota(jnp.int32, (tile, count), 0)
        delta_row = lax.div(key, cols) + row_off - lax.div(query, cols)
        delta_col = lax.rem(key, cols) + col_off - lax.rem(query, cols)
        near = delta_row * delta_row + delta_col * delta_col <= RADIUS * RADIUS
        limit = jnp.where(valid, 0.0, MASKED)
        bias[:, first : first + count] = jnp.where(near, limit, MASKED)

    region(0, tile, 0, 0, True)
    region(tile, tile, 0, -cols, has_left)
    region(2 * tile, tile, 0, cols, has_right)
    for way in range(2):
        row_off = -RADIUS if way == 0 else rows
        for piece in range(3):
            col_off = (0, -cols, cols)[piece]
            first = 3 * tile + (3 * way + piece) * strip
            region(first, strip, row_off, col_off, strip_in[way] & piece_there[piece])

            @pl.when(jnp.logical_not(strip_in[way] & piece_there[piece]))
            def _():
                for _, dst in images:
                    dst[first : first + strip, :] = jnp.zeros((strip, dst.shape[1]), dst.dtype)

        @pl.when(jnp.logical_not(side_in[way]))
        def _():
            for _, dst in images:
                first = tile * (1 + way)
                dst[first : first + tile, :] = jnp.zeros((tile, dst.shape[1]), dst.dtype)

    def text_bias():
        return jnp.where(lax.broadcasted_iota(jnp.int32, (1, text), 1) < length_ref[0], 0.0, MASKED)

    def attend_chunk(c):
        limit = text_bias()

        def one_head(j, carry):
            column = pl.ds(pl.multiple_of(c * cc + j * HEAD_DIM, 128), HEAD_DIM)
            query = q_ref[:, column]
            score_win = dot_nt(query, kbuf[:, column]) + bias[...]
            score_text = dot_nt(query, tk[:, column]) + limit
            peak = jnp.maximum(
                jnp.max(score_win, axis=1, keepdims=True), jnp.max(score_text, axis=1, keepdims=True)
            )
            weight_win = jnp.exp2((score_win - peak) * SCALE)
            weight_text = jnp.exp2((score_text - peak) * SCALE)
            total = jnp.sum(weight_win, axis=1, keepdims=True) + jnp.sum(weight_text, axis=1, keepdims=True)
            numer = dot_nn(weight_win.astype(jnp.bfloat16), vbuf[:, column])
            numer = numer + dot_nn(weight_text.astype(jnp.bfloat16), tv[:, column])
            image_out[:, column] = (numer / total).astype(jnp.bfloat16)
            return carry

        lax.fori_loop(0, chunk_heads, one_head, 0, unroll=2)

    block = math.gcd(text, 128)

    def text_partial(b, carry):
        block_rows = pl.ds(pl.multiple_of(b * block, block), block)
        lane = lax.broadcasted_iota(jnp.int32, (block, 128), 1)
        stats = jnp.zeros((block, 128), jnp.float32)
        for j in range(part_heads):
            column = slice(j * HEAD_DIM, (j + 1) * HEAD_DIM)
            score = dot_nt(tq[block_rows, column], xk[:, column])
            peak = jnp.max(score, axis=1, keepdims=True)
            weight = jnp.exp2((score - peak) * SCALE)
            total = jnp.sum(weight, axis=1, keepdims=True)
            obuf[block_rows, column] = dot_nn(weight.astype(jnp.bfloat16), xv[:, column])
            stats = jnp.where(lane == j, peak, jnp.where(lane == 64 + j, total, stats))
        obuf[block_rows, pc : pc + 128] = stats
        return carry

    o_sends = []
    for g in range(groups):
        for d in range(n_w):
            if g or d:
                to_w = lax.rem(w + d, n_w)
                their_rows = pl.ds(pl.multiple_of(to_w * own_text, 16), own_text)
                at_slot = g * n_w + d
                o_sends.append(
                    send(
                        obuf.at[their_rows, :],
                        rbuf.at[at_slot],
                        os_.at[at_slot],
                        or_.at[at_slot],
                        at(lax.rem(h + g * parts, n_h), to_w),
                    )
                )

    f_sends = [
        send(
            tout.at[:, part_cols],
            tout.at[:, part_cols],
            fs.at[d],
            fr.at[d],
            at(group * parts + lax.rem(part + d, parts), w),
        )
        for d in range(1, parts)
    ]

    def text_combine():
        limit = text_bias()
        for j in range(part_heads):
            column = slice(j * HEAD_DIM, (j + 1) * HEAD_DIM)
            wide = pl.ds(pl.multiple_of(part * pc + j * HEAD_DIM, 128), HEAD_DIM)
            score = dot_nt(tq[my_rows, column], tk[:, wide]) + limit
            own_peak = jnp.max(score, axis=1, keepdims=True)
            pieces = [(obuf[my_rows, column], obuf[my_rows, pc : pc + 128])]
            for s in range(1, groups * n_w):
                pieces.append((rbuf[s, :, column], rbuf[s, :, pc : pc + 128]))
            peak = own_peak
            for _, stats in pieces:
                peak = jnp.maximum(peak, stats[:, j : j + 1])
            weight = jnp.exp2((score - peak) * SCALE)
            total = jnp.sum(weight, axis=1, keepdims=True)
            numer = dot_nn(weight.astype(jnp.bfloat16), tv[:, wide])
            for value, stats in pieces:
                factor = jnp.exp2((stats[:, j : j + 1] - peak) * SCALE)
                total = total + factor * stats[:, 64 + j : 65 + j]
                numer = numer + factor * value
            tout[:, wide] = (numer / total).astype(jnp.bfloat16)

    for i in range(2):
        locals_[i].wait()
    for c in range(CHUNKS):
        relay_chunk(c)
        if c + 2 < CHUNKS:
            start_chunk(c + 2)
        if c == 0:
            for copy in q_sends + x_sends:
                copy.wait_recv()
            for i in range(2, 5):
                locals_[i].wait()
            lax.fori_loop(0, text // block, text_partial, 0)
            for copy in o_sends:
                copy.start()
        else:
            wait_chunk(c - 1)
            attend_chunk(c - 1)
    last = CHUNKS - 1
    for copy in pair_sends(last):
        copy.wait_recv()
    for copy in o_sends:
        copy.wait_recv()
    text_combine()
    for copy in f_sends:
        copy.start()
    for way in range(2):
        for piece in range(3):

            @pl.when(strip_in[way] & piece_there[piece])
            def _(way=way, piece=piece):
                for copy in strip_sends(last, way, piece):
                    copy.wait_recv()

    attend_chunk(last)
    for copy in f_sends:
        copy.wait_recv()
    text_out[...] = tout[...]
    for copy in q_sends + x_sends + o_sends + f_sends:
        copy.wait_send()
    for c in range(CHUNKS):
        finish_chunk(c)


def shards(image_query, image_key, image_value, text_query, text_key, text_value, text_length):
    rows, cols, width = image_query.shape
    heads = width // HEAD_DIM
    n_h, n_w = lax.axis_size("height"), lax.axis_size("width")
    own_text = text_query.shape[0]
    parts = math.gcd(heads, n_h)
    tile = rows * cols
    strip = RADIUS * cols
    text = own_text * n_w
    sources = (n_h // parts) * n_w
    pc = width // parts
    keys = 3 * tile + 6 * strip
    bf16, f32 = jnp.bfloat16, jnp.float32
    dma = pltpu.SemaphoreType.DMA
    any_spec = pl.BlockSpec(memory_space=pl.ANY)
    vmem_spec = pl.BlockSpec(memory_space=pltpu.VMEM)
    image_out, text_out = pl.pallas_call(
        functools.partial(joint, (n_h, n_w, rows, cols, heads, own_text, parts)),
        out_shape=(
            jax.ShapeDtypeStruct((tile, width), bf16),
            jax.ShapeDtypeStruct((own_text, width), bf16),
        ),
        in_specs=[pl.BlockSpec(memory_space=pltpu.SMEM), vmem_spec] + [any_spec] * 5,
        out_specs=(vmem_spec, vmem_spec),
        scratch_shapes=[
            pltpu.VMEM((keys, width), bf16),
            pltpu.VMEM((keys, width), bf16),
            pltpu.VMEM((text, width), bf16),
            pltpu.VMEM((text, width), bf16),
            pltpu.VMEM((text, pc), bf16),
            pltpu.VMEM((parts * tile, pc), bf16),
            pltpu.VMEM((parts * tile, pc), bf16),
            pltpu.VMEM((text, pc + 128), f32),
            pltpu.VMEM((sources, own_text, pc + 128), f32),
            pltpu.VMEM((own_text, width), bf16),
            pltpu.VMEM((tile, keys), f32),
            dma((5 + 2 * CHUNKS,)),
            dma((CHUNKS, 2, 2)),
            dma((CHUNKS, 2, 2)),
            dma((CHUNKS, 2, 3, 2)),
            dma((CHUNKS, 2, 3, 2)),
            dma((CHUNKS, n_w, 2)),
            dma((CHUNKS, n_w, 2)),
            dma((CHUNKS, 2)),
            dma((CHUNKS, 2)),
            dma((n_w,)),
            dma((n_w,)),
            dma((parts, 2)),
            dma((parts, 2)),
            dma((sources,)),
            dma((sources,)),
            dma((parts,)),
            dma((parts,)),
        ],
        compiler_params=pltpu.CompilerParams(
            collective_id=0, has_side_effects=True, vmem_limit_bytes=50 * 1024 * 1024
        ),
        cost_estimate=pl.CostEstimate(
            flops=4 * tile * (keys + 2 * text) * width,
            bytes_accessed=12 * tile * width,
            transcendentals=heads * tile * (keys + 2 * text),
        ),
        name="joint_attention",
    )(
        text_length,
        image_query.reshape(tile, width),
        image_key.reshape(tile, width),
        image_value.reshape(tile, width),
        text_query,
        text_key,
        text_value,
    )
    return image_out.reshape(rows, cols, width), text_out


def solution(mesh):
    in_specs = (
        P(("batch", "height"), "width", None),
        P(("batch", "height"), "width", None),
        P(("batch", "height"), "width", None),
        P(("batch", "width"), None),
        P(("batch", "width"), None),
        P(("batch", "width"), None),
        P("batch"),
    )
    out_specs = (P(("batch", "height"), "width", None), P(("batch", "width"), None))
    return jax.shard_map(shards, mesh=mesh, in_specs=in_specs, out_specs=out_specs, check_vma=False)
```

time: 386 us -> 122 us (0.32)
  the two profiles are of different devices: /device:TPU:0 before, /device:TPU:17 now
where the time goes in v1:
time: 122 us; the launch traced here: 121 us
  Pallas kernels  113 us (93%)
  local copies, waits for them, and re-layouts  6.87 us (6%)
  between operations  1.3 us (1%)
    pallas_call x1, Pallas kernels, shards(): pl.pallas_call(functools.partial(joint, (n_h, n_w, rows, cols, heads, own...  113 us
    unnamed x12, local copies, waits for them, and re-layouts  6.87 us

profile of v1, /device:TPU:17, one launch (start us, length us, event | category | flops | bytes accessed | tf_op | source)
XLA Modules:
  0.0 121.3 jit_solution(10915362609334235073)
XLA Ops:
  1.3 0.0 copy-start
  1.3 1.1 copy-done
  2.4 0.0 copy-start.1
  2.4 1.1 copy-done.1
  3.5 0.0 copy-start.2
  3.5 1.0 copy-done.2
  4.5 0.0 copy-start.3
  4.5 1.0 copy-done.3
  5.5 0.0 copy-start.4
  5.5 1.0 copy-done.4
  6.5 113.1 %joint_attention.1 = (bf16[128,3072]{1,0:T(8,128)(2,1)S(1)}, bf16[64,3072]{1,0:T(8,128)(2,1)S(1)}) custom-call(s32[1]{0:T(128)S(6)} %copy.11.length_ref, bf16[128,3072]{1,0:T(8,128)(2,1)S(1)} %bitcast.5, bf16[128,3072]{1,0:T(8,128)(2,1)S(1)} %bitcast.6, bf16[128,3072]{1,0:T(8,128)(2,1)} %bitcast.7, bf16[64,3072]{1,0:T(8,128)(2,1)S(1)} %copy-done.2, ...), custom_call_target="tpu_custom_call" | custom-call | flops 2013265920 | bytes 4718592 | tf_op jit(solution)/shard_map/joint_attention/pallas_call | solution.py:460
  119.7 0.9 copy.12
  120.6 0.7 copy.13
Async XLA Ops:
  1.3 1.1 copy-start
  2.4 1.1 copy-start.1
  3.5 1.0 copy-start.2
  4.5 1.0 copy-start.3
  5.5 1.0 copy-start.4

commit v2 on v1

--- a/solution.py
+++ b/solution.py
@@ -12,6 +12,7 @@
 RADIUS = 8
 CHUNKS = 4
 MASKED = -1e30
+VMEM_BYTES = 62 * 1024 * 1024
 SCALE = math.log2(math.e) / math.sqrt(HEAD_DIM)
 NT = (((1,), (1,)), ((), ()))
 
@@ -27,7 +28,7 @@
 def joint(
     dims,
     length_ref,
-    q_ref,
+    q_hbm,
     k_hbm,
     v_hbm,
     tq_hbm,
@@ -35,6 +36,7 @@
     tv_hbm,
     image_out,
     text_out,
+    q_ref,
     kbuf,
     vbuf,
     tk,
@@ -55,8 +57,6 @@
     tr,
     ps,
     pr,
-    qs,
-    qr,
     xs,
     xr,
     os_,
@@ -122,28 +122,64 @@
     locals_ = []
     for i, (src, dst) in enumerate(images):
         locals_.append(pltpu.make_async_copy(src, dst.at[pl.ds(0, tile), :], local_sem.at[i]))
-    locals_.append(pltpu.make_async_copy(tq_hbm.at[:, part_cols], tq.at[my_rows, :], local_sem.at[2]))
     my_slot = pl.ds(pl.multiple_of(part * tile, 16), tile)
     for i, (src, dst) in enumerate(((k_hbm, xk), (v_hbm, xv))):
-        locals_.append(pltpu.make_async_copy(src.at[:, part_cols], dst.at[my_slot, :], local_sem.at[3 + i]))
-
-    def half_cols(c):
-        return pl.ds(pl.multiple_of(c * cc + par * hc, 128), hc)
-
-    for c in range(CHUNKS):
-        for i, (src, dst) in enumerate(texts):
-            locals_.append(
-                pltpu.make_async_copy(
-                    src.at[:, half_cols(c)], dst.at[my_rows, half_cols(c)], local_sem.at[5 + 2 * c + i]
-                )
-            )
+        locals_.append(pltpu.make_async_copy(src.at[:, part_cols], dst.at[my_slot, :], local_sem.at[2 + i]))
+
+    slabs = ((tq_hbm, tq, pl.ds(0, pc)), (tk_hbm, tk, part_cols), (tv_hbm, tv, part_cols))
+    for i, (src, dst, columns) in enumerate(slabs):
+        locals_.append(pltpu.make_async_copy(src.at[:, part_cols], dst.at[my_rows, columns], local_sem.at[4 + i]))
+    locals_.append(pltpu.make_async_copy(q_hbm, q_ref, local_sem.at[7]))
     for copy in locals_:
         copy.start()
 
-    q_sends = [
-        send(tq_hbm.at[:, part_cols], tq.at[my_rows, :], qs.at[d], qr.at[d], at(h, lax.rem(w + d, n_w)))
-        for d in range(1, n_w)
-    ]
+    def slab_sends(hop, way):
+        owner = w - hop if way == 0 else w + hop
+        owner_rows = pl.ds(pl.multiple_of(owner * own_text, 16), own_text)
+        to = w + 1 if way == 0 else w - 1
+        return [
+            send(
+                src.at[:, part_cols] if hop == 0 else dst.at[owner_rows, columns],
+                dst.at[owner_rows, columns],
+                ts.at[hop, way, i],
+                tr.at[hop, way, i],
+                at(h, to),
+            )
+            for i, (src, dst, columns) in enumerate(slabs)
+        ]
+
+    def slab_in(hop, way):
+        return w > hop if way == 0 else w < n_w - 1 - hop
+
+    def flipped(bit):
+        return part + bit * (1 - 2 * lax.rem(lax.div(part, bit), 2))
+
+    exchanges = []
+    offsets = [0]
+    bit = parts // 2
+    while bit:
+        stage = []
+        for offset in offsets:
+            held = part
+            for b in range(8):
+                if offset & (1 << b):
+                    held = held + (1 << b) * (1 - 2 * lax.rem(lax.div(part, 1 << b), 2))
+            columns = pl.ds(pl.multiple_of(held * pc, 128), pc)
+            for i, (_, dst) in enumerate(texts):
+                at_sem = len(offsets) + len(stage) // 2
+                stage.append(
+                    send(
+                        dst.at[:, columns],
+                        dst.at[:, columns],
+                        ps.at[at_sem, i],
+                        pr.at[at_sem, i],
+                        at(group * parts + flipped(bit), w),
+                    )
+                )
+        exchanges.append(stage)
+        offsets = offsets + [o ^ bit for o in offsets]
+        bit //= 2
+
     x_sends = []
     for d in range(1, parts):
         other = lax.rem(part + d, parts)
@@ -152,26 +188,6 @@
             x_sends.append(
                 send(src.at[:, other_cols], dst.at[my_slot, :], xs.at[d, i], xr.at[d, i], at(group * parts + other, w))
             )
-
-    def text_sends(c):
-        return [
-            send(
-                src.at[:, half_cols(c)],
-                dst.at[my_rows, half_cols(c)],
-                ts.at[c, d, i],
-                tr.at[c, d, i],
-                at(h, lax.rem(w + d, n_w)),
-            )
-            for d in range(1, n_w)
-            for i, (src, dst) in enumerate(texts)
-        ]
-
-    def pair_sends(c):
-        partner = h + 1 - 2 * par
-        return [
-            send(dst.at[:, half_cols(c)], dst.at[:, half_cols(c)], ps.at[c, i], pr.at[c, i], at(partner, w))
-            for i, (_, dst) in enumerate(texts)
-        ]
 
     def side_sends(c, way):
         to = w + 1 if way == 0 else w - 1
@@ -210,8 +226,6 @@
     piece_there = (True, has_left, has_right)
 
     def start_chunk(c):
-        for copy in text_sends(c):
-            copy.start()
         for way in range(2):
 
             @pl.when(side_out[way])
@@ -225,12 +239,6 @@
                     copy.start()
 
     def relay_chunk(c):
-        for copy in text_sends(c):
-            copy.wait_recv()
-        for i in range(2):
-            locals_[5 + 2 * c + i].wait()
-        for copy in pair_sends(c):
-            copy.start()
         for way in range(2):
 
             @pl.when(side_in[way])
@@ -245,8 +253,6 @@
                             copy.start()
 
     def wait_chunk(c):
-        for copy in pair_sends(c):
-            copy.wait_recv()
         for way in range(2):
             for piece in range(3):
 
@@ -256,8 +262,6 @@
                         copy.wait_recv()
 
     def finish_chunk(c):
-        for copy in text_sends(c) + pair_sends(c):
-            copy.wait_send()
         for way in range(2):
 
             @pl.when(side_out[way])
@@ -272,7 +276,14 @@
                     for copy in strip_sends(c, way, piece):
                         copy.wait_send()
 
-    for copy in q_sends + x_sends:
+    for way in range(2):
+
+        @pl.when(side_out[way])
+        def _(way=way):
+            for copy in slab_sends(0, way):
+                copy.start()
+
+    for copy in x_sends:
         copy.start()
     start_chunk(0)
     start_chunk(1)
@@ -343,9 +354,14 @@
             peak = jnp.max(score, axis=1, keepdims=True)
             weight = jnp.exp2((score - peak) * SCALE)
             total = jnp.sum(weight, axis=1, keepdims=True)
-            obuf[block_rows, column] = dot_nn(weight.astype(jnp.bfloat16), xv[:, column])
-            stats = jnp.where(lane == j, peak, jnp.where(lane == 64 + j, total, stats))
-        obuf[block_rows, pc : pc + 128] = stats
+            numer = dot_nn(weight.astype(jnp.bfloat16), xv[:, column])
+            obuf[block_rows, column] = (numer / total).astype(jnp.bfloat16)
+            log_total = peak * SCALE + jnp.log2(total)
+            for third in range(3):
+                piece = log_total.astype(jnp.bfloat16).astype(jnp.float32)
+                stats = jnp.where(lane == 32 * third + j, piece, stats)
+                log_total = log_total - piece
+        obuf[block_rows, pc : pc + 128] = stats.astype(jnp.bfloat16)
         return carry
 
     o_sends = []
@@ -382,61 +398,100 @@
             column = slice(j * HEAD_DIM, (j + 1) * HEAD_DIM)
             wide = pl.ds(pl.multiple_of(part * pc + j * HEAD_DIM, 128), HEAD_DIM)
             score = dot_nt(tq[my_rows, column], tk[:, wide]) + limit
-            own_peak = jnp.max(score, axis=1, keepdims=True)
             pieces = [(obuf[my_rows, column], obuf[my_rows, pc : pc + 128])]
             for s in range(1, groups * n_w):
                 pieces.append((rbuf[s, :, column], rbuf[s, :, pc : pc + 128]))
-            peak = own_peak
+            logs = []
             for _, stats in pieces:
-                peak = jnp.maximum(peak, stats[:, j : j + 1])
-            weight = jnp.exp2((score - peak) * SCALE)
+                stats = stats.astype(jnp.float32)
+                logs.append(stats[:, j : j + 1] + stats[:, 32 + j : 33 + j] + stats[:, 64 + j : 65 + j])
+            peak = jnp.max(score, axis=1, keepdims=True) * SCALE
+            for log_total in logs:
+                peak = jnp.maximum(peak, log_total)
+            weight = jnp.exp2(score * SCALE - peak)
             total = jnp.sum(weight, axis=1, keepdims=True)
             numer = dot_nn(weight.astype(jnp.bfloat16), tv[:, wide])
-            for value, stats in pieces:
-                factor = jnp.exp2((stats[:, j : j + 1] - peak) * SCALE)
-                total = total + factor * stats[:, 64 + j : 65 + j]
-                numer = numer + factor * value
+            for (value, _), log_total in zip(pieces, logs):
+                factor = jnp.exp2(log_total - peak)
+                total = total + factor
+                numer = numer + factor * value.astype(jnp.float32)
             tout[:, wide] = (numer / total).astype(jnp.bfloat16)
 
-    for i in range(2):
-        locals_[i].wait()
-    for c in range(CHUNKS):
-        relay_chunk(c)
-        if c + 2 < CHUNKS:
-            start_chunk(c + 2)
-        if c == 0:
-            for copy in q_sends + x_sends:
+    for copy in locals_:
+        copy.wait()
+    for hop in range(n_w - 1):
+        for way in range(2):
+
+            @pl.when(slab_in(hop, way))
+            def _(way=way, hop=hop):
+                for copy in slab_sends(hop, way):
+                    copy.wait_recv()
+
+            if hop + 1 < n_w - 1:
+
+                @pl.when(slab_in(hop, way) & side_out[way])
+                def _(way=way, hop=hop):
+                    for copy in slab_sends(hop + 1, way):
+                        copy.start()
+
+    def run_exchange(k):
+        if k > 0:
+            for copy in exchanges[k - 1]:
                 copy.wait_recv()
-            for i in range(2, 5):
-                locals_[i].wait()
-            lax.fori_loop(0, text // block, text_partial, 0)
-            for copy in o_sends:
+        if k < len(exchanges):
+            for copy in exchanges[k]:
                 copy.start()
-        else:
-            wait_chunk(c - 1)
-            attend_chunk(c - 1)
-    last = CHUNKS - 1
-    for copy in pair_sends(last):
+
+    run_exchange(0)
+    relay_chunk(0)
+    start_chunk(2)
+    for copy in x_sends:
         copy.wait_recv()
+    lax.fori_loop(0, text // block, text_partial, 0)
+    for copy in o_sends:
+        copy.start()
+    run_exchange(1)
+    relay_chunk(1)
+    start_chunk(3)
+    for k in range(2, len(exchanges) + 1):
+        run_exchange(k)
+    wait_chunk(0)
+    attend_chunk(0)
+    relay_chunk(2)
+    wait_chunk(1)
+    attend_chunk(1)
+    relay_chunk(3)
     for copy in o_sends:
         copy.wait_recv()
     text_combine()
     for copy in f_sends:
         copy.start()
-    for way in range(2):
-        for piece in range(3):
-
-            @pl.when(strip_in[way] & piece_there[piece])
-            def _(way=way, piece=piece):
-                for copy in strip_sends(last, way, piece):
-                    copy.wait_recv()
-
-    attend_chunk(last)
+    wait_chunk(2)
+    attend_chunk(2)
+    wait_chunk(3)
+    attend_chunk(3)
     for copy in f_sends:
         copy.wait_recv()
     text_out[...] = tout[...]
-    for copy in q_sends + x_sends + o_sends + f_sends:
+    for stage in exchanges:
+        for copy in stage:
+            copy.wait_send()
+    for copy in x_sends + o_sends + f_sends:
         copy.wait_send()
+    for way in range(2):
+
+        @pl.when(side_out[way])
+        def _(way=way):
+            for copy in slab_sends(0, way):
+                copy.wait_send()
+
+        for hop in range(1, n_w - 1):
+
+            @pl.when(slab_in(hop - 1, way) & side_out[way])
+            def _(way=way, hop=hop):
+                for copy in slab_sends(hop, way):
+                    copy.wait_send()
+
     for c in range(CHUNKS):
         finish_chunk(c)
 
@@ -446,7 +501,7 @@
     heads = width // HEAD_DIM
     n_h, n_w = lax.axis_size("height"), lax.axis_size("width")
     own_text = text_query.shape[0]
-    parts = math.gcd(heads, n_h)
+    parts = math.gcd(math.gcd(heads, n_h), 8)
     tile = rows * cols
     strip = RADIUS * cols
     text = own_text * n_w
@@ -463,9 +518,10 @@
             jax.ShapeDtypeStruct((tile, width), bf16),
             jax.ShapeDtypeStruct((own_text, width), bf16),
         ),
-        in_specs=[pl.BlockSpec(memory_space=pltpu.SMEM), vmem_spec] + [any_spec] * 5,
+        in_specs=[pl.BlockSpec(memory_space=pltpu.SMEM)] + [any_spec] * 6,
         out_specs=(vmem_spec, vmem_spec),
         scratch_shapes=[
+            pltpu.VMEM((tile, width), bf16),
             pltpu.VMEM((keys, width), bf16),
             pltpu.VMEM((keys, width), bf16),
             pltpu.VMEM((text, width), bf16),
@@ -473,21 +529,19 @@
             pltpu.VMEM((text, pc), bf16),
             pltpu.VMEM((parts * tile, pc), bf16),
             pltpu.VMEM((parts * tile, pc), bf16),
-            pltpu.VMEM((text, pc + 128), f32),
-            pltpu.VMEM((sources, own_text, pc + 128), f32),
+            pltpu.VMEM((text, pc + 128), bf16),
+            pltpu.VMEM((sources, own_text, pc + 128), bf16),
             pltpu.VMEM((own_text, width), bf16),
             pltpu.VMEM((tile, keys), f32),
-            dma((5 + 2 * CHUNKS,)),
+            dma((8,)),
             dma((CHUNKS, 2, 2)),
             dma((CHUNKS, 2, 2)),
             dma((CHUNKS, 2, 3, 2)),
             dma((CHUNKS, 2, 3, 2)),
-            dma((CHUNKS, n_w, 2)),
-            dma((CHUNKS, n_w, 2)),
-            dma((CHUNKS, 2)),
-            dma((CHUNKS, 2)),
-            dma((n_w,)),
-            dma((n_w,)),
+            dma((n_w, 2, 3)),
+            dma((n_w, 2, 3)),
+            dma((parts, 2)),
+            dma((parts, 2)),
             dma((parts, 2)),
             dma((parts, 2)),
             dma((sources,)),
@@ -496,7 +550,7 @@
             dma((parts,)),
         ],
         compiler_params=pltpu.CompilerParams(
-            collective_id=0, has_side_effects=True, vmem_limit_bytes=50 * 1024 * 1024
+            collective_id=0, has_side_effects=True, vmem_limit_bytes=VMEM_BYTES
         ),
         cost_estimate=pl.CostEstimate(
             flops=4 * tile * (keys + 2 * text) * width,

time: 122 us -> 87.7 us (0.72)
  the two profiles are of different devices: /device:TPU:17 before, /device:TPU:0 now
where the time goes in v2:
time: 87.7 us; the launch traced here: 86.8 us
  Pallas kernels  82.7 us (94%)
  local copies, waits for them, and re-layouts  2.86 us (3%)
  between operations  1.3 us (1%)
    pallas_call x1, Pallas kernels, shards(): pl.pallas_call(functools.partial(joint, (n_h, n_w, rows, cols, heads, own...  82.7 us
    unnamed x4, local copies, waits for them, and re-layouts  2.86 us

profile of v2, /device:TPU:0, one launch (start us, length us, event | category | flops | bytes accessed | tf_op | source)
XLA Modules:
  0.0 86.8 jit_solution(16295228595089327950)
XLA Ops:
  1.3 82.7 %joint_attention.1 = (bf16[128,3072]{1,0:T(8,128)(2,1)}, bf16[64,3072]{1,0:T(8,128)(2,1)}) custom-call(s32[1]{0:T(128)S(6)} %copy.11.length_ref, bf16[128,3072]{1,0:T(8,128)(2,1)} %bitcast.5, bf16[128,3072]{1,0:T(8,128)(2,1)} %bitcast.6, bf16[128,3072]{1,0:T(8,128)(2,1)} %bitcast.7, bf16[64,3072]{1,0:T(8,128)(2,1)} %tq_hbm.1, bf16[64,3072]{1,0:T(8,128)(2,1)} %tk_hbm.1, ...), custom_call_target="tpu_custom_call" | custom-call | flops 2013265920 | bytes 4718592 | tf_op jit(solution)/shard_map/joint_attention/pallas_call | solution.py:515
  83.9 0.0 copy-start
  84.0 2.1 %copy.12 = bf16[16,8,3072]{2,1,0:T(8,128)(2,1)} copy(bf16[16,8,3072]{2,1,0:T(8,128)(2,1)} %bitcast.4) | data formatting | bytes 1572864
  86.1 0.0 copy-done
  86.1 0.7 copy.13
Async XLA Ops:
  83.9 2.1 %copy-start = (bf16[64,3072]{1,0:T(8,128)(2,1)S(1)}, bf16[64,3072]{1,0:T(8,128)(2,1)}, u32[]{:S(2)}) copy-start(bf16[64,3072]{1,0:T(8,128)(2,1)} %get-tuple-element.9) | copy-start | bytes 1179652

commit v3 on v2

--- a/solution.py
+++ b/solution.py
@@ -23,6 +23,12 @@
 
 def dot_nn(a, b):
     return jnp.dot(a, b, preferred_element_type=jnp.float32)
+
+
+def dot_split(weight, value):
+    high = weight.astype(jnp.bfloat16)
+    low = (weight - high.astype(jnp.float32)).astype(jnp.bfloat16)
+    return dot_nn(high, value) + dot_nn(low, value)
 
 
 def joint(
@@ -286,7 +292,6 @@
     for copy in x_sends:
         copy.start()
     start_chunk(0)
-    start_chunk(1)
 
     def region(first, count, row_off, col_off, valid):
         key = lax.broadcasted_iota(jnp.int32, (tile, count), 1)
@@ -354,7 +359,7 @@
             peak = jnp.max(score, axis=1, keepdims=True)
             weight = jnp.exp2((score - peak) * SCALE)
             total = jnp.sum(weight, axis=1, keepdims=True)
-            numer = dot_nn(weight.astype(jnp.bfloat16), xv[:, column])
+            numer = dot_split(weight, xv[:, column])
             obuf[block_rows, column] = (numer / total).astype(jnp.bfloat16)
             log_total = peak * SCALE + jnp.log2(total)
             for third in range(3):
@@ -410,7 +415,7 @@
                 peak = jnp.maximum(peak, log_total)
             weight = jnp.exp2(score * SCALE - peak)
             total = jnp.sum(weight, axis=1, keepdims=True)
-            numer = dot_nn(weight.astype(jnp.bfloat16), tv[:, wide])
+            numer = dot_split(weight, tv[:, wide])
             for (value, _), log_total in zip(pieces, logs):
                 factor = jnp.exp2(log_total - peak)
                 total = total + factor
@@ -433,6 +438,11 @@
                 def _(way=way, hop=hop):
                     for copy in slab_sends(hop + 1, way):
                         copy.start()
+
+        if hop + 1 < CHUNKS:
+            start_chunk(hop + 1)
+    for c in range(n_w, CHUNKS):
+        start_chunk(c)
 
     def run_exchange(k):
         if k > 0:
@@ -444,7 +454,6 @@
 
     run_exchange(0)
     relay_chunk(0)
-    start_chunk(2)
     for copy in x_sends:
         copy.wait_recv()
     lax.fori_loop(0, text // block, text_partial, 0)
@@ -452,7 +461,6 @@
         copy.start()
     run_exchange(1)
     relay_chunk(1)
-    start_chunk(3)
     for k in range(2, len(exchanges) + 1):
         run_exchange(k)
     wait_chunk(0)

time: 87.7 us -> 85.8 us (0.978)
  Pallas kernels: 82.7 us -> 80.7 us
    pallas_call x1, Pallas kernels: 82.7 us -> 80.7 us  [shards(): pl.pallas_call(functools.partial(joint, (n_h, n_w, rows, cols, heads, own...]
where the time goes in v3:
time: 85.8 us; the launch traced here: 84.9 us
  Pallas kernels  80.7 us (94%)
  local copies, waits for them, and re-layouts  2.86 us (3%)
  between operations  1.3 us (2%)
    pallas_call x1, Pallas kernels, shards(): pl.pallas_call(functools.partial(joint, (n_h, n_w, rows, cols, heads, own...  80.7 us
    unnamed x4, local copies, waits for them, and re-layouts  2.86 us

profile of v3, /device:TPU:0, one launch (start us, length us, event | category | flops | bytes accessed | tf_op | source)
XLA Modules:
  0.0 84.9 jit_solution(17455380166263474016)
XLA Ops:
  1.3 80.7 %joint_attention.1 = (bf16[128,3072]{1,0:T(8,128)(2,1)}, bf16[64,3072]{1,0:T(8,128)(2,1)}) custom-call(s32[1]{0:T(128)S(6)} %copy.11.length_ref, bf16[128,3072]{1,0:T(8,128)(2,1)} %bitcast.5, bf16[128,3072]{1,0:T(8,128)(2,1)} %bitcast.6, bf16[128,3072]{1,0:T(8,128)(2,1)} %bitcast.7, bf16[64,3072]{1,0:T(8,128)(2,1)} %tq_hbm.1, bf16[64,3072]{1,0:T(8,128)(2,1)} %tk_hbm.1, ...), custom_call_target="tpu_custom_call" | custom-call | flops 2013265920 | bytes 4718592 | tf_op jit(solution)/shard_map/joint_attention/pallas_call | solution.py:523
  82.0 0.0 copy-start
  82.0 2.1 %copy.12 = bf16[16,8,3072]{2,1,0:T(8,128)(2,1)} copy(bf16[16,8,3072]{2,1,0:T(8,128)(2,1)} %bitcast.4) | data formatting | bytes 1572864
  84.1 0.0 copy-done
  84.1 0.7 copy.13
Async XLA Ops:
  82.0 2.1 %copy-start = (bf16[64,3072]{1,0:T(8,128)(2,1)S(1)}, bf16[64,3072]{1,0:T(8,128)(2,1)}, u32[]{:S(2)}) copy-start(bf16[64,3072]{1,0:T(8,128)(2,1)} %get-tuple-element.9) | copy-start | bytes 1179652
